TPU v7x, 256 devices: a whole 4x4x8 slice. The times are simulated.
256 devices in a mesh: slab: 32 (over y_hi, z, core), pencil: 8 (over y_lo, x).
Axes of the slice: x: 4, y: 4 (y_hi: 2, y_lo: 2; y = y_hi * 2 + y_lo), z: 8, core: 2. Of those that a mesh axis runs over, the one named last changes fastest.
Arguments:
- sources: float32 [4, 262144], P(None, ('slab', 'pencil')), may hold values from -6 to 6
- proj_weight: float32 [262144, 128], P(('slab', 'pencil')), may hold values from -1.5 to 1.5
- tri_slot: int32 [262144], P(('slab', 'pencil')), may hold values from 0 to 127, as said below
- cell_block: int32 [32768], P(('slab', 'pencil')), may hold values from 0 to 131071, as said below
- green: float32 [256, 256, 256], P('slab', 'pencil'), may hold values from -6 to 6
- near_index: int32 [16, 262144], P(None, ('slab', 'pencil')), may hold values from 0 to 1023
- near_coef: float32 [2, 16, 262144], P(None, None, ('slab', 'pencil')), may hold values from -2 to 2
Outputs:
- adjoint_potential: float32 [4, 262144], P(None, ('slab', 'pencil'))
Inputs may be any that keep to these rules, and one draw needn't show every extreme that they name: `tri_slot`: in each group of 1024 consecutive triangles, the slots named for pencil column q are exactly q * 16 to q * 16 + n - 1 for some n of 1 to 16; in every group the last column has n = 16. `cell_block`: cell slot c of group g = c // 128 names a block inside slab g // P and pencil column (c // 16) % P of the grid, where P is the size of the pencil axis and slab i holds grid rows i * 256 // Q onward (Q the size of the slab axis), column j grid columns j * 256 // P onward; in each column, slot 0 names the lowest block of that region and slot 1 the highest.
All inputs are finite; a program needn't handle non-finite values.
Results may differ from a plain program's by a relative error of at most 0.000054.
Values sent between devices are 32-bit elements; how exact they have to be, the bound alone decides.
No kernel may reach another device: no remote copies, remote signals or barrier semaphores. Data moves between devices by JAX's collectives and lax.ppermute only.
A program may use at most 128 MiB of HBM per device.

v0:
```python
import math

import jax
import jax.numpy as jnp
import numpy as np
from jax import lax
from jax.experimental import pallas as pl
from jax.experimental.pallas import tpu as pltpu
from jax.sharding import PartitionSpec as P

f32 = jnp.float32
bf16 = jnp.bfloat16
BOTH = ("slab", "pencil")
LANES = 128
struct = jax.ShapeDtypeStruct


def call(body, out_shape, scratch=(), mib=24, cost=(0, 0), in_specs=None):
    more = {} if in_specs is None else {"in_specs": in_specs}
    return pl.pallas_call(
        body,
        out_shape=out_shape,
        scratch_shapes=list(scratch),
        compiler_params=pltpu.CompilerParams(vmem_limit_bytes=mib << 20),
        cost_estimate=pl.CostEstimate(flops=cost[0], bytes_accessed=cost[1], transcendentals=0),
        **more,
    )


def halves(x):
    high = x.astype(bf16)
    return high, (x - high.astype(f32)).astype(bf16)


def dot(a, b, dims=((1,), (0,))):
    return lax.dot_general(a, b, (dims, ((), ())), preferred_element_type=f32)


def table_dot(table, x):
    t_high, t_low = table
    high, low = halves(x)
    m = t_high.shape[0]
    both = dot(jnp.concatenate([t_high, t_low], axis=0), high)
    return both[:m] + (both[m:] + dot(t_high, low))


def dot_table(x, table):
    m = x.shape[0]
    high, low = halves(x)
    both = dot(jnp.concatenate([high, low], axis=0), table[0])
    return both[:m] + (both[m:] + dot(high, table[1]))


def complex_table(rows, row_part, columns, column_part, n, inverse):
    angle = (np.outer(rows, columns) % n) * (2.0 * math.pi / n)
    sine = np.sin(angle) * np.where(row_part == 0, 1.0, -1.0)[:, None]
    if inverse:
        sine = -sine
    same = row_part[:, None] == column_part[None, :]
    return np.where(same, np.cos(angle), sine) / (n if inverse else 1)


def tables(n):
    half = n // 2
    part, z = np.arange(n) // half, np.arange(n) % half
    kz = [2 * z + p for p in range(2)]
    b2, slab, x_part, b1, b0 = (a.reshape(-1) for a in np.indices((2, 16, 2, 2, 2)))
    x = slab * 8 + b2 * 4 + b1 * 2 + b0
    kx_part, kx_high, kx_slab = (a.reshape(-1) for a in np.indices((2, 4, 32)))
    kx = [kx_slab * 8 + kx_high * 2 + p for p in range(2)]
    y = z // 32 * 32 + z % 8 * 4 + z // 8 % 4
    ky = [z // 16 * 32 + z % 16 * 2 + p for p in range(2)]

    def both(make):
        return jnp.asarray(np.stack([make(p) for p in range(2)]).astype(np.float32))

    return (
        both(lambda p: complex_table(kz[p], part, z, part, n, False)),
        both(lambda p: complex_table(kx[p], kx_part, x, x_part, n, False)),
        both(lambda p: complex_table(ky[p], part, y, part, n, False).T),
        both(lambda p: complex_table(y, part, ky[p], part, n, True).T),
        both(lambda p: complex_table(x, x_part, kx[p], kx_part, n, True)),
        both(lambda p: complex_table(z, part, kz[p], part, n, True)),
    )


def green_order(n):
    place = np.arange(n)
    kx = place // 64 % 2 + place // 16 % 4 * 2
    ky = place % 16 * 2 + place // 128
    return jnp.asarray((kx[:, None] * 32 + ky[:, None] == place[None, :]).astype(np.float32))


def lane_iota(rows):
    return lax.broadcasted_iota(jnp.int32, (rows, LANES), 1)


def swap_bits(parts, distances):
    parts = list(parts)
    lane = lane_iota(parts[0].shape[0])
    for level, distance in enumerate(distances):
        stride = len(parts) >> (level + 1)
        bit = (lane & distance) != 0
        for low in range(len(parts)):
            if low & stride == 0:
                a, b = parts[low], parts[low | stride]
                moved = jnp.where(bit, a, b)
                if distance == LANES // 2:
                    moved = pltpu.roll(moved, distance, 1)
                else:
                    moved = jnp.take_along_axis(moved, lane ^ distance, axis=1)
                parts[low], parts[low | stride] = jnp.where(bit, moved, a), jnp.where(bit, b, moved)
    return parts


def block_column(block, x_blocks, y_blocks, z_blocks):
    z = block % z_blocks
    y = block // z_blocks % 64 % y_blocks
    x = block // (z_blocks * 64) % x_blocks
    return z // 8 * LANES + x * 64 + z % 8 * 8 + y


def charges_kernel(src_hbm, w_hbm, slot_hbm, block_hbm, msg_ref, src_ref, w_ref, slot_ref, block_ref, sems):
    channels, tris = src_ref.shape
    pairs = [(src_hbm, src_ref), (slot_hbm, slot_ref), (block_hbm, block_ref), (w_hbm, w_ref)]
    copies = [pltpu.make_async_copy(a, b, sems.at[i]) for i, (a, b) in enumerate(pairs)]
    for copy in copies:
        copy.start()
    for copy in copies[:3]:
        copy.wait()
    slots = block_ref.shape[1]
    pencils = msg_ref.shape[0] - channels * slots
    cap = slots // pencils
    rows = channels * cap + 1
    place = block_column(block_ref[...], 2, 8, 32).astype(f32)
    for q in range(pencils):
        row = place if q == 0 else pltpu.roll(place, slots - q * cap, 1)
        msg_ref[q * rows + rows - 1 : (q + 1) * rows, :] = row
    hit = lax.broadcasted_iota(jnp.int32, (slots, tris), 0) == slot_ref[...]
    hit = jnp.where(hit, 1.0, 0.0).astype(bf16)
    left = [jnp.concatenate([hit * half[c : c + 1, :] for c in range(channels)], axis=0) for half in halves(src_ref[...])]
    for copy in copies[3:]:
        copy.wait()
    w_high, w_low = halves(w_ref[...])
    both = dot(left[0], jnp.concatenate([w_high, w_low], axis=1))
    total = both[:, :LANES] + (both[:, LANES:] + dot(left[1], w_high))
    for c in range(channels):
        for q in range(pencils):
            msg_ref[q * rows + c * cap : q * rows + (c + 1) * cap, :] = total[
                c * slots + q * cap : c * slots + (q + 1) * cap
            ]


def tiles_of(part, g, x_1, x_0):
    blocks, grid = [], []
    for m in range(8):
        wave, y_low = m // 4, m % 4
        stencil = (x_1 * 2 + x_0) * 4 + y_low
        blocks.append(((part * 2 + wave) * LANES + stencil * 8, g * LANES))
        grid.append((part * 128 + (g * 8 + m) * 8, (x_1 * 2 + x_0) * LANES))
    return blocks, grid


GROUPS = [(part, g, x_1, x_0) for part in range(2) for g in range(2) for x_1 in range(2) for x_0 in range(2)]


def tile(ref, row, column):
    return ref[row : row + 8, column : column + LANES]


def forward_kernel(got_ref, green_ref, table_ref, msg_ref, hit_ref, placed_ref, z_ref):
    cells = hit_ref.shape[1]
    channels = 4
    pencils = got_ref.shape[0] - channels * cells
    cap = cells // pencils
    rows = channels * cap + 1
    place = jnp.concatenate(
        [jnp.broadcast_to(got_ref[(q + 1) * rows - 1 : (q + 1) * rows, :], (cap, LANES)) for q in range(pencils)], axis=0
    )
    own = lane_iota(cells) == lax.broadcasted_iota(jnp.int32, (cells, LANES), 0) % cap
    place = jnp.sum(jnp.where(own, place, 0.0), axis=1, keepdims=True)
    place = jnp.broadcast_to(place, (cells, LANES))
    upper = place >= 2 * LANES
    at = jnp.where(upper, place - 2 * LANES, place)
    lane = lane_iota(cells).astype(f32)
    marks = [jnp.where(lane + g * LANES == at, 1.0, 0.0) for g in range(2)]
    hit = jnp.concatenate(marks + [jnp.where(upper, -mark, mark) for mark in marks], axis=1)
    hit_ref[...] = hit.T.astype(bf16)
    hit = hit.astype(bf16)
    charge = jnp.concatenate(
        [
            jnp.concatenate(
                [got_ref[q * rows + c * cap : q * rows + (c + 1) * cap, :] for q in range(pencils)], axis=0
            ).T
            for c in range(channels)
        ],
        axis=0,
    )
    placed_ref[...] = dot(jnp.concatenate(halves(charge), axis=1), jnp.concatenate([hit, hit], axis=0))
    for group in GROUPS:
        blocks, grid = tiles_of(*group)
        for p in range(2):
            found = swap_bits([tile(placed_ref, r, c + p * 2 * LANES) for r, c in blocks], (32, 16, 8))
            for (r, c), moved in zip(grid, found):
                z_ref[p, r : r + 8, c : c + LANES] = moved
    half = msg_ref.shape[0] // 20
    for p in range(2):
        spec = table_dot((table_ref[p, 0], table_ref[p, 1]), z_ref[p])
        for row in range(8):
            part, x = row // 4, row % 4
            msg_ref[pl.ds(p * 10 + row, half, 20), :] = spec[
                part * half : (part + 1) * half, x * LANES : (x + 1) * LANES
            ]
    for row in range(2):
        msg_ref[pl.ds(8 + row, 2 * half, 10), :] = green_ref[:, row * LANES : (row + 1) * LANES]


def plane_kernel(got_ref, xf_ref, yf_ref, yi_ref, xi_ref, msg_ref):
    n = got_ref.shape[0] // 10
    half = n // 2
    got = got_ref.reshape(32, 8, 10, LANES)
    green = []
    for r in range(2):
        parts = [got[:, j, 8 + r, :] for j in range(8)]
        found = jnp.concatenate(swap_bits(parts, (64, 32, 16)), axis=0)
        green.append(jnp.concatenate([found, found], axis=1))
    tiles = [got[:, j, :8, :].reshape(n, LANES) for j in range(8)]
    by_x = [[t[:half] + t[half:] for t in tiles], [t[:half] - t[half:] for t in tiles]]
    spec = []
    for p in range(2):
        low, high = by_x[p][:4], by_x[p][4:]
        found = [
            swap_bits([u + v for u, v in zip(low, high)], (64, 32)),
            swap_bits([u - v for u, v in zip(low, high)], (64, 32)),
        ]
        rows = [
            jnp.concatenate([found[q][x_2 * 2 + w] for w in range(2) for q in range(2)], axis=1) for x_2 in range(2)
        ]
        spec.append(table_dot(halves(xf_ref[p]), jnp.concatenate(rows, axis=0)))
    sums = []
    for q in range(2):
        rows = [
            jnp.concatenate(
                [spec[p][part * half : (part + 1) * half, (w * 2 + q) * LANES : (w * 2 + q + 1) * LANES] for part in range(2)],
                axis=1,
            )
            for w in range(2)
            for p in range(2)
        ]
        result = dot_table(jnp.concatenate(rows, axis=0), halves(yf_ref[q]))
        result = result * jnp.concatenate([green[q], green[q]], axis=0)
        sums.append(dot_table(result, halves(yi_ref[q])))
    plane = []
    for p in range(2):
        rows = [
            jnp.concatenate(
                [
                    sums[q][(w * 2 + p) * half : (w * 2 + p + 1) * half, part * half : (part + 1) * half]
                    for w in range(2)
                    for q in range(2)
                ],
                axis=1,
            )
            for part in range(2)
        ]
        plane.append(table_dot(halves(xi_ref[p]), jnp.concatenate(rows, axis=0)))
    msg = msg_ref.reshape(32, 8, 8, LANES)
    for upper in range(2):
        moved = []
        for q in range(2):
            parts = []
            for x_2 in range(2):
                for w in range(2):
                    even, odd = [
                        o[x_2 * half : (x_2 + 1) * half, (w * 2 + q) * LANES : (w * 2 + q + 1) * LANES] for o in plane
                    ]
                    parts.append(even - odd if upper else even + odd)
            moved.append(swap_bits(parts, (64, 32)))
        for j in range(4):
            for j_2 in range(2):
                part = moved[0][j] - moved[1][j] if j_2 else moved[0][j] + moved[1][j]
                msg[upper * 16 : (upper + 1) * 16, j_2 * 4 + j, :, :] = part.reshape(16, 8, LANES)


def inverse_kernel(got_ref, hit_ref, table_ref, msg_ref, z_ref, a_ref):
    n = got_ref.shape[0] // 8
    pencils = msg_ref.shape[0]
    cells = hit_ref.shape[1]
    cap = cells // pencils
    half = n // 2
    for p in range(2):
        rows = [
            jnp.concatenate([got_ref[pl.ds(p * 8 + part * 4 + x, half, 16), :] for x in range(4)], axis=1)
            for part in range(2)
        ]
        z_ref[p] = table_dot(halves(table_ref[p]), jnp.concatenate(rows, axis=0))
    for group in GROUPS:
        blocks, grid = tiles_of(*group)
        for p in range(2):
            found = swap_bits([tile(z_ref.at[p], r, c) for r, c in grid], (32, 16, 8))
            for (r, c), moved in zip(blocks, found):
                a_ref[r : r + 8, c + p * 2 * LANES : c + (p * 2 + 1) * LANES] = moved
    picked = dot(jnp.concatenate(halves(a_ref[...]), axis=0), hit_ref[...])
    rows = 4 * LANES
    for c in range(4):
        cells_c = picked[c * LANES : (c + 1) * LANES] + picked[rows + c * LANES : rows + (c + 1) * LANES]
        msg_ref[:, c * cap : (c + 1) * cap, :] = cells_c.T.reshape(pencils, cap, LANES)


def near_kernel(
    src_ref, table_ref, index_ref, coef_ref, w_ref, slot_ref, green_ref, order_ref, z_ref, near_ref, wt_ref, hit_ref, out_ref, split_ref
):
    channels = src_ref.shape[0]
    near, tris = index_ref.shape
    for start in range(0, tris, LANES):
        cols = slice(start, start + LANES)
        total = [jnp.zeros((8, LANES), f32) for _ in range(channels)]
        for top in range(0, near, 8):
            index = index_ref[top : top + 8, cols]
            lane, row = index & (LANES - 1), index >> 7
            got = [jnp.zeros((8, LANES), f32) for _ in range(channels)]
            for r in range(8):
                hit = row == r
                for c in range(channels):
                    line = jnp.broadcast_to(table_ref[c, r : r + 1, :], (8, LANES))
                    got[c] = jnp.where(hit, jnp.take_along_axis(line, lane, axis=1), got[c])
            a = coef_ref[0, top : top + 8, cols]
            b = coef_ref[1, top : top + 8, cols]
            for w in range(channels // 2):
                re, im = got[w], got[w + channels // 2]
                total[w] += a * re - b * im
                total[w + channels // 2] += a * im + b * re
        for c in range(channels):
            near_ref[c : c + 1, cols] = jnp.sum(total[c], axis=0, keepdims=True)
    wt_ref[...] = w_ref[...].T
    hit = lax.broadcasted_iota(jnp.int32, hit_ref.shape, 0) == slot_ref[...]
    hit_ref[...] = jnp.where(hit, 1.0, 0.0).astype(bf16)
    order = order_ref[...].astype(bf16)
    high, low = halves(green_ref[...])
    out_ref[...] = (dot(order, high) + dot(order, low)).T
    for p in range(2):
        split_ref[p, 0], split_ref[p, 1] = halves(z_ref[p])


def far_kernel(got_ref, hit_ref, wt_ref, near_ref, out_ref):
    pencils, rows, _ = got_ref.shape
    channels, tris = near_ref.shape
    cap = rows // channels
    slots = pencils * cap
    hit = hit_ref[...]
    values = jnp.concatenate(
        [got_ref[:, c * cap : (c + 1) * cap, :].reshape(slots, LANES).T for c in range(channels)], axis=0
    )
    picked = dot(jnp.concatenate(halves(values), axis=1), jnp.concatenate([hit, hit], axis=0))
    wt = wt_ref[...]
    for c in range(channels):
        far = jnp.sum(picked[c * LANES : (c + 1) * LANES] * wt, axis=0, keepdims=True)
        out_ref[c : c + 1, :] = far + near_ref[c : c + 1, :]


def exchange(x, axis):
    parts = lax.axis_size(axis)
    sent = x.reshape(parts, 1, x.size // parts)
    return lax.all_to_all(sent, axis, split_axis=0, concat_axis=0, tiled=True).reshape(x.shape)


def per_device(sources, proj_weight, tri_slot, cell_block, green, near_index, near_coef):
    slabs, pencils = lax.axis_size("slab"), lax.axis_size("pencil")
    channels, tris = sources.shape
    slots = cell_block.shape[0]
    cap = slots // pencils
    n = green.shape[2]
    devices = slabs * pencils
    zf, xf, yf, yi, xi, zi = tables(n)
    slot_row = tri_slot.reshape(1, tris)
    block_row = cell_block.reshape(1, slots)

    msg = call(
        charges_kernel,
        struct((pencils * (channels * cap + 1), LANES), f32),
        scratch=[
            pltpu.VMEM((channels, tris), f32),
            pltpu.VMEM((tris, LANES), f32),
            pltpu.VMEM((1, tris), jnp.int32),
            pltpu.VMEM((1, slots), jnp.int32),
            pltpu.SemaphoreType.DMA((4,)),
        ],
        in_specs=[pl.BlockSpec(memory_space=pltpu.HBM)] * 4,
        mib=60,
    )(sources, proj_weight, slot_row, block_row)
    near, wt, tri_hit, green_rows, zf = call(
        near_kernel,
        (
            struct((channels, tris), f32),
            struct((LANES, tris), f32),
            struct((slots, tris), bf16),
            struct((n, n), f32),
            struct((2, 2, n, n), bf16),
        ),
        cost=(1 << 30, 1 << 20),
    )(sources, sources.reshape(channels, 8, LANES), near_index, near_coef, proj_weight, slot_row, green.reshape(n, n), green_order(n), zf)
    got = exchange(msg, "pencil")
    got, near, wt, tri_hit, green_rows, zf = lax.optimization_barrier((got, near, wt, tri_hit, green_rows, zf))
    msg, hit = call(
        forward_kernel,
        (struct((devices * 10, LANES), f32), struct((512, slots), bf16)),
        scratch=[pltpu.VMEM((channels * LANES, 512), f32), pltpu.VMEM((2, n, 512), f32)],
    )(got, green_rows, zf)
    got = exchange(msg, BOTH)
    msg = call(plane_kernel, struct((devices * 8, LANES), f32))(got, xf, yf, yi, xi)
    got = exchange(msg, BOTH)
    msg = call(
        inverse_kernel,
        struct((pencils, channels * cap, LANES), f32),
        scratch=[pltpu.VMEM((2, n, 512), f32), pltpu.VMEM((channels * LANES, 512), f32)],
    )(got, hit, zi)
    got = exchange(msg, "pencil")
    return call(far_kernel, struct((channels, tris), f32))(got, tri_hit, wt, near)


def solution(mesh):
    return jax.shard_map(
        per_device,
        mesh=mesh,
        in_specs=(
            P(None, BOTH),
            P(BOTH, None),
            P(BOTH),
            P(BOTH),
            P("slab", "pencil", None),
            P(None, BOTH),
            P(None, None, BOTH),
        ),
        out_specs=P(None, BOTH),
        check_vma=False,
    )
```

profile of v0, /device:TPU:1, one launch (start us, length us, event | category | flops | bytes accessed | tf_op | source)
XLA Modules:
  0.0 119.9 jit_solution(4343472119136377888)
XLA Ops:
  0.0 0.0 copy-start.12
  0.0 0.0 copy-start.6
  0.0 0.0 copy-start.4
  0.0 0.0 copy-start.7
  0.0 0.0 copy-start.9
  0.0 0.0 copy-start.10
  0.0 0.0 copy-start.8
  0.0 2.6 %shard_map.136 = f32[520,128]{1,0:T(8,128)} custom-call(f32[4,1024]{1,0:T(4,128)} %src_ref.1, f32[1024,128]{1,0:T(8,128)} %w_ref.1, s32[1,1024]{1,0:T(1,128)} %bitcast.24, s32[1,128]{1,0:T(1,128)} %bitcast.28), custom_call_target="tpu_custom_call" | custom-call | tf_op jit(solution)/shard_map/pallas_call | solution.py:378
  2.7 5.9 %all-to-all-start = ((f32[8,1,8320]{2,1,0:T(1,128)}), f32[8,1,8320]{2,1,0:T(1,128)S(1)}, u32[]{:S(2)}, u32[]{:S(2)}) async-start(f32[8,1,8320]{2,1,0:T(1,128)} %bitcast.27), calls=%async_computation | async-start | bytes 532480 | tf_op jit(solution)/shard_map/all_to_all | solution.py:364
  8.5 0.0 copy-done.6
  8.5 0.0 copy-done.12
  8.6 0.0 copy-done.4
  8.6 0.0 copy-done.7
  8.6 0.0 copy-done.9
  8.6 0.0 copy-done.10
  8.6 0.0 copy-done.8
  8.6 0.0 copy-start.11
  8.6 1.0 copy-done.11
  9.6 1.0 shard_map.137
  10.7 4.2 %all-to-all-done = f32[8,1,8320]{2,1,0:T(1,128)S(1)} async-done(((f32[8,1,8320]{2,1,0:T(1,128)}), f32[8,1,8320]{2,1,0:T(1,128)S(1)}, u32[]{:S(2)}, u32[]{:S(2)}) %all-to-all-start) | async-done | bytes 266272 | tf_op jit(solution)/shard_map/all_to_all | solution.py:364
  14.9 1.3 %shard_map.138 = (f32[2560,128]{1,0:T(8,128)S(1)}, bf16[512,128]{1,0:T(8,128)(2,1)S(1)}) custom-call(f32[520,128]{1,0:T(8,128)S(1)} %bitcast.19, f32[256,256]{1,0:T(8,128)S(1)} %get-tuple-element.24.green_ref, bf16[2,2,256,256]{3,2,1,0:T(8,128)(2,1)S(1)} %get-tuple-element.25.table_ref), custom_call_target="tpu_custom_call" | custom-call | tf_op jit(solution)/shard_map/pallas_call | solution.py:404
  16.1 0.0 copy-start
  16.2 0.0 copy-start.1
  16.2 0.0 copy-start.2
  16.2 0.0 copy-start.3
  16.2 50.1 %all_to_all.20 = f32[256,1,1280]{2,1,0:T(1,128)S(1)} all-to-all(f32[256,1,1280]{2,1,0:T(1,128)S(1)} %bitcast.18), channel_id=1, replica_groups=mesh['slab'=32,'pencil'=8] {'slab','pencil'}, dimensions={0} | all-to-all | bytes 2621440 | tf_op jit(solution)/shard_map/all_to_all | solution.py:364
  66.3 0.0 copy-done
  66.3 0.0 copy-done.1
  66.3 0.0 copy-done.2
  66.3 0.0 copy-done.3
  66.3 3.0 %shard_map.139 = f32[2048,128]{1,0:T(8,128)S(1)} custom-call(f32[2560,128]{1,0:T(8,128)S(1)} %bitcast.15, f32[2,256,256]{2,1,0:T(8,128)S(1)} %copy-done.3, f32[2,256,256]{2,1,0:T(8,128)S(1)} %copy-done.2, f32[2,256,256]{2,1,0:T(8,128)S(1)} %copy-done.1, f32[2,256,256]{2,1,0:T(8,128)S(1)} %copy-done), custom_call_target="tpu_custom_call" | custom-call | tf_op jit(solution)/shard_map/pallas_call | solution.py:410
  69.4 0.0 copy-start.5
  69.4 36.3 %all_to_all.21 = f32[256,1,1024]{2,1,0:T(1,128)S(1)} all-to-all(f32[256,1,1024]{2,1,0:T(1,128)S(1)} %bitcast.16), channel_id=1, replica_groups=mesh['slab'=32,'pencil'=8] {'slab','pencil'}, dimensions={0} | all-to-all | bytes 2097152 | tf_op jit(solution)/shard_map/all_to_all | solution.py:364
  105.6 0.0 copy-done.5
  105.6 1.5 %shard_map.140 = f32[8,64,128]{2,1,0:T(8,128)S(1)} custom-call(f32[2048,128]{1,0:T(8,128)S(1)} %bitcast.17, bf16[512,128]{1,0:T(8,128)(2,1)S(1)} %get-tuple-element.27.hit_ref, f32[2,256,256]{2,1,0:T(8,128)S(1)} %copy-done.5), custom_call_target="tpu_custom_call" | custom-call | tf_op jit(solution)/shard_map/pallas_call | solution.py:412
  107.2 11.6 %all_to_all.22 = f32[8,1,8192]{2,1,0:T(1,128)S(1)} all-to-all(f32[8,1,8192]{2,1,0:T(1,128)S(1)} %bitcast.20), channel_id=1, replica_groups=mesh['slab'=32,'pencil'=8] {'pencil'}, dimensions={0} | all-to-all | bytes 524288 | tf_op jit(solution)/shard_map/all_to_all | solution.py:364
  118.8 1.1 shard_map.141
  (1 shorter events, 0.0 us)
Async XLA Ops:
  0.0 8.5 %copy-start.12 = (f32[256,256]{1,0:T(8,128)S(1)}, f32[256,256]{1,0:T(8,128)}, u32[]{:S(2)}) copy-start(f32[256,256]{1,0:T(8,128)} %constant.20.clone.order_ref) | copy-start | bytes 786436
  0.0 8.5 %copy-start.6 = (f32[4,1024]{1,0:T(4,128)S(1)}, f32[4,1024]{1,0:T(4,128)}, u32[]{:S(2)}) copy-start(f32[4,1024]{1,0:T(4,128)} %src_ref.1) | copy-start | bytes 49156
  0.0 8.6 %copy-start.4 = (f32[1024,128]{1,0:T(8,128)S(1)}, f32[1024,128]{1,0:T(8,128)}, u32[]{:S(2)}) copy-start(f32[1024,128]{1,0:T(8,128)} %w_ref.1) | copy-start | bytes 1572868
  0.0 8.6 %copy-start.7 = (s32[1024]{0:T(1024)S(1)}, s32[1024]{0:T(1024)}, u32[]{:S(2)}) copy-start(s32[1024]{0:T(1024)} %param.16) | copy-start | bytes 12292
  0.0 8.6 %copy-start.9 = (f32[2,16,1024]{2,1,0:T(8,128)S(1)}, f32[2,16,1024]{2,1,0:T(8,128)}, u32[]{:S(2)}) copy-start(f32[2,16,1024]{2,1,0:T(8,128)} %coef_ref.1) | copy-start | bytes 393220
  0.0 8.6 %copy-start.10 = (s32[16,1024]{1,0:T(8,128)S(1)}, s32[16,1024]{1,0:T(8,128)}, u32[]{:S(2)}) copy-start(s32[16,1024]{1,0:T(8,128)} %index_ref.1) | copy-start | bytes 196612
  0.0 8.6 %copy-start.8 = (f32[8,32,256]{2,1,0:T(8,128)S(1)}, f32[8,32,256]{2,1,0:T(8,128)}, u32[]{:S(2)}) copy-start(f32[8,32,256]{2,1,0:T(8,128)} %param.18) | copy-start | bytes 786436
  2.7 12.2 %all-to-all-start = ((f32[8,1,8320]{2,1,0:T(1,128)}), f32[8,1,8320]{2,1,0:T(1,128)S(1)}, u32[]{:S(2)}, u32[]{:S(2)}) async-start(f32[8,1,8320]{2,1,0:T(1,128)} %bitcast.27), calls=%async_computation | async-start | bytes 532480 | tf_op jit(solution)/shard_map/all_to_all | solution.py:364
  8.6 1.0 copy-start.11
  16.1 50.2 %copy-start = (f32[2,256,256]{2,1,0:T(8,128)S(1)}, f32[2,256,256]{2,1,0:T(8,128)}, u32[]{:S(2)}) copy-start(f32[2,256,256]{2,1,0:T(8,128)} %constant.18.clone.xi_ref) | copy-start | bytes 1572868
  16.2 50.2 %copy-start.1 = (f32[2,256,256]{2,1,0:T(8,128)S(1)}, f32[2,256,256]{2,1,0:T(8,128)}, u32[]{:S(2)}) copy-start(f32[2,256,256]{2,1,0:T(8,128)} %constant.17.clone.yi_ref) | copy-start | bytes 1572868
  16.2 50.2 %copy-start.2 = (f32[2,256,256]{2,1,0:T(8,128)S(1)}, f32[2,256,256]{2,1,0:T(8,128)}, u32[]{:S(2)}) copy-start(f32[2,256,256]{2,1,0:T(8,128)} %constant.16.clone.yf_ref) | copy-start | bytes 1572868
  16.2 50.2 %copy-start.3 = (f32[2,256,256]{2,1,0:T(8,128)S(1)}, f32[2,256,256]{2,1,0:T(8,128)}, u32[]{:S(2)}) copy-start(f32[2,256,256]{2,1,0:T(8,128)} %constant.15.clone.xf_ref) | copy-start | bytes 1572868
  69.4 36.3 %copy-start.5 = (f32[2,256,256]{2,1,0:T(8,128)S(1)}, f32[2,256,256]{2,1,0:T(8,128)}, u32[]{:S(2)}) copy-start(f32[2,256,256]{2,1,0:T(8,128)} %constant.19.clone.table_ref) | copy-start | bytes 1572868
where the time goes:
time: 120 us
  blocking collectives  98 us (82%)
  Pallas kernels  10.6 us (9%)
  starting transfers between devices  5.87 us (5%)
  waiting for transfers between devices  4.17 us (3%)
    all_to_all x3, blocking collectives, exchange(): lax.all_to_all(sent, axis, split_axis=0, concat_axis=0, tiled=True)  98 us
    all_to_all x1, starting transfers between devices, exchange(): lax.all_to_all(sent, axis, split_axis=0, concat_axis=0, tiled=True)  5.87 us
    all_to_all x1, waiting for transfers between devices, exchange(): lax.all_to_all(sent, axis, split_axis=0, concat_axis=0, tiled=True)  4.17 us
    pallas_call x1, Pallas kernels, per_device(): call(plane_kernel, struct((devices * 8, LANES), f32))(got, xf, yf, yi, xi)  3.01 us
    pallas_call x1, Pallas kernels, per_device(): call(charges_kernel, struct((pencils * (channels * cap + 1), LANES), f32)...  2.6 us
  transfers between devices with their start and end apart: 1, of which 1 were waited for; matrix products, arithmetic and copies ran while one was open for 0% of the time, Pallas kernels for 1%

commit v1 on v0

--- a/solution.py
+++ b/solution.py
@@ -124,10 +124,13 @@
     channels, tris = src_ref.shape
     pairs = [(src_hbm, src_ref), (slot_hbm, slot_ref), (block_hbm, block_ref), (w_hbm, w_ref)]
     copies = [pltpu.make_async_copy(a, b, sems.at[i]) for i, (a, b) in enumerate(pairs)]
-    for copy in copies:
-        copy.start()
-    for copy in copies[:3]:
-        copy.wait()
+    for i in (1, 3, 0, 2):
+        copies[i].start()
+    copies[1].wait()
+    hit = lax.broadcasted_iota(jnp.int32, (block_ref.shape[1], tris), 0) == slot_ref[...]
+    hit = jnp.where(hit, 1.0, 0.0).astype(bf16)
+    copies[0].wait()
+    copies[2].wait()
     slots = block_ref.shape[1]
     pencils = msg_ref.shape[0] - channels * slots
     cap = slots // pencils
@@ -136,8 +139,6 @@
     for q in range(pencils):
         row = place if q == 0 else pltpu.roll(place, slots - q * cap, 1)
         msg_ref[q * rows + rows - 1 : (q + 1) * rows, :] = row
-    hit = lax.broadcasted_iota(jnp.int32, (slots, tris), 0) == slot_ref[...]
-    hit = jnp.where(hit, 1.0, 0.0).astype(bf16)
     left = [jnp.concatenate([hit * half[c : c + 1, :] for c in range(channels)], axis=0) for half in halves(src_ref[...])]
     for copy in copies[3:]:
         copy.wait()

time: 120 us -> 120 us (level)
  no operation moved by 1% of the time
where the time goes in v1:
time: 120 us
  blocking collectives  98 us (82%)
  Pallas kernels  10.6 us (9%)
  starting transfers between devices  5.87 us (5%)
  waiting for transfers between devices  4.17 us (3%)
    all_to_all x3, blocking collectives, exchange(): lax.all_to_all(sent, axis, split_axis=0, concat_axis=0, tiled=True)  98 us
    all_to_all x1, starting transfers between devices, exchange(): lax.all_to_all(sent, axis, split_axis=0, concat_axis=0, tiled=True)  5.87 us
    all_to_all x1, waiting for transfers between devices, exchange(): lax.all_to_all(sent, axis, split_axis=0, concat_axis=0, tiled=True)  4.17 us
    pallas_call x1, Pallas kernels, per_device(): call(plane_kernel, struct((devices * 8, LANES), f32))(got, xf, yf, yi, xi)  3 us
    pallas_call x1, Pallas kernels, per_device(): call(charges_kernel, struct((pencils * (channels * cap + 1), LANES), f32)...  2.59 us
  transfers between devices with their start and end apart: 1, of which 1 were waited for; matrix products, arithmetic and copies ran while one was open for 0% of the time, Pallas kernels for 1%

profile of v1, /device:TPU:1, one launch (start us, length us, event | category | flops | bytes accessed | tf_op | source)
XLA Modules:
  0.0 119.9 jit_solution(8914806893280893322)
XLA Ops:
  0.0 0.0 copy-start.12
  0.0 0.0 copy-start.6
  0.0 0.0 copy-start.4
  0.0 0.0 copy-start.7
  0.0 0.0 copy-start.9
  0.0 0.0 copy-start.10
  0.0 0.0 copy-start.8
  0.0 2.6 %shard_map.136 = f32[520,128]{1,0:T(8,128)} custom-call(f32[4,1024]{1,0:T(4,128)} %src_ref.1, f32[1024,128]{1,0:T(8,128)} %w_ref.1, s32[1,1024]{1,0:T(1,128)} %bitcast.24, s32[1,128]{1,0:T(1,128)} %bitcast.28), custom_call_target="tpu_custom_call" | custom-call | tf_op jit(solution)/shard_map/pallas_call | solution.py:379
  2.6 5.9 %all-to-all-start = ((f32[8,1,8320]{2,1,0:T(1,128)}), f32[8,1,8320]{2,1,0:T(1,128)S(1)}, u32[]{:S(2)}, u32[]{:S(2)}) async-start(f32[8,1,8320]{2,1,0:T(1,128)} %bitcast.27), calls=%async_computation | async-start | bytes 532480 | tf_op jit(solution)/shard_map/all_to_all | solution.py:365
  8.5 0.0 copy-done.6
  8.5 0.0 copy-done.12
  8.6 0.0 copy-done.4
  8.6 0.0 copy-done.7
  8.6 0.0 copy-done.9
  8.6 0.0 copy-done.10
  8.6 0.0 copy-done.8
  8.6 0.0 copy-start.11
  8.6 1.0 copy-done.11
  9.6 1.0 shard_map.137
  10.7 4.2 %all-to-all-done = f32[8,1,8320]{2,1,0:T(1,128)S(1)} async-done(((f32[8,1,8320]{2,1,0:T(1,128)}), f32[8,1,8320]{2,1,0:T(1,128)S(1)}, u32[]{:S(2)}, u32[]{:S(2)}) %all-to-all-start) | async-done | bytes 266272 | tf_op jit(solution)/shard_map/all_to_all | solution.py:365
  14.9 1.3 %shard_map.138 = (f32[2560,128]{1,0:T(8,128)S(1)}, bf16[512,128]{1,0:T(8,128)(2,1)S(1)}) custom-call(f32[520,128]{1,0:T(8,128)S(1)} %bitcast.19, f32[256,256]{1,0:T(8,128)S(1)} %get-tuple-element.24.green_ref, bf16[2,2,256,256]{3,2,1,0:T(8,128)(2,1)S(1)} %get-tuple-element.25.table_ref), custom_call_target="tpu_custom_call" | custom-call | tf_op jit(solution)/shard_map/pallas_call | solution.py:405
  16.1 0.0 copy-start
  16.1 0.0 copy-start.1
  16.2 0.0 copy-start.2
  16.2 0.0 copy-start.3
  16.2 50.1 %all_to_all.20 = f32[256,1,1280]{2,1,0:T(1,128)S(1)} all-to-all(f32[256,1,1280]{2,1,0:T(1,128)S(1)} %bitcast.18), channel_id=1, replica_groups=mesh['slab'=32,'pencil'=8] {'slab','pencil'}, dimensions={0} | all-to-all | bytes 2621440 | tf_op jit(solution)/shard_map/all_to_all | solution.py:365
  66.3 0.0 copy-done
  66.3 0.0 copy-done.1
  66.3 0.0 copy-done.2
  66.3 0.0 copy-done.3
  66.3 3.0 %shard_map.139 = f32[2048,128]{1,0:T(8,128)S(1)} custom-call(f32[2560,128]{1,0:T(8,128)S(1)} %bitcast.15, f32[2,256,256]{2,1,0:T(8,128)S(1)} %copy-done.3, f32[2,256,256]{2,1,0:T(8,128)S(1)} %copy-done.2, f32[2,256,256]{2,1,0:T(8,128)S(1)} %copy-done.1, f32[2,256,256]{2,1,0:T(8,128)S(1)} %copy-done), custom_call_target="tpu_custom_call" | custom-call | tf_op jit(solution)/shard_map/pallas_call | solution.py:411
  69.3 0.0 copy-start.5
  69.4 36.3 %all_to_all.21 = f32[256,1,1024]{2,1,0:T(1,128)S(1)} all-to-all(f32[256,1,1024]{2,1,0:T(1,128)S(1)} %bitcast.16), channel_id=1, replica_groups=mesh['slab'=32,'pencil'=8] {'slab','pencil'}, dimensions={0} | all-to-all | bytes 2097152 | tf_op jit(solution)/shard_map/all_to_all | solution.py:365
  105.6 0.0 copy-done.5
  105.6 1.6 %shard_map.140 = f32[8,64,128]{2,1,0:T(8,128)S(1)} custom-call(f32[2048,128]{1,0:T(8,128)S(1)} %bitcast.17, bf16[512,128]{1,0:T(8,128)(2,1)S(1)} %get-tuple-element.27.hit_ref, f32[2,256,256]{2,1,0:T(8,128)S(1)} %copy-done.5), custom_call_target="tpu_custom_call" | custom-call | tf_op jit(solution)/shard_map/pallas_call | solution.py:413
  107.2 11.6 %all_to_all.22 = f32[8,1,8192]{2,1,0:T(1,128)S(1)} all-to-all(f32[8,1,8192]{2,1,0:T(1,128)S(1)} %bitcast.20), channel_id=1, replica_groups=mesh['slab'=32,'pencil'=8] {'pencil'}, dimensions={0} | all-to-all | bytes 524288 | tf_op jit(solution)/shard_map/all_to_all | solution.py:365
  118.8 1.1 shard_map.141
  (1 shorter events, 0.0 us)
Async XLA Ops:
  0.0 8.5 %copy-start.12 = (f32[256,256]{1,0:T(8,128)S(1)}, f32[256,256]{1,0:T(8,128)}, u32[]{:S(2)}) copy-start(f32[256,256]{1,0:T(8,128)} %constant.20.clone.order_ref) | copy-start | bytes 786436
  0.0 8.5 %copy-start.6 = (f32[4,1024]{1,0:T(4,128)S(1)}, f32[4,1024]{1,0:T(4,128)}, u32[]{:S(2)}) copy-start(f32[4,1024]{1,0:T(4,128)} %src_ref.1) | copy-start | bytes 49156
  0.0 8.5 %copy-start.4 = (f32[1024,128]{1,0:T(8,128)S(1)}, f32[1024,128]{1,0:T(8,128)}, u32[]{:S(2)}) copy-start(f32[1024,128]{1,0:T(8,128)} %w_ref.1) | copy-start | bytes 1572868
  0.0 8.6 %copy-start.7 = (s32[1024]{0:T(1024)S(1)}, s32[1024]{0:T(1024)}, u32[]{:S(2)}) copy-start(s32[1024]{0:T(1024)} %param.16) | copy-start | bytes 12292
  0.0 8.6 %copy-start.9 = (f32[2,16,1024]{2,1,0:T(8,128)S(1)}, f32[2,16,1024]{2,1,0:T(8,128)}, u32[]{:S(2)}) copy-start(f32[2,16,1024]{2,1,0:T(8,128)} %coef_ref.1) | copy-start | bytes 393220
  0.0 8.6 %copy-start.10 = (s32[16,1024]{1,0:T(8,128)S(1)}, s32[16,1024]{1,0:T(8,128)}, u32[]{:S(2)}) copy-start(s32[16,1024]{1,0:T(8,128)} %index_ref.1) | copy-start | bytes 196612
  0.0 8.6 %copy-start.8 = (f32[8,32,256]{2,1,0:T(8,128)S(1)}, f32[8,32,256]{2,1,0:T(8,128)}, u32[]{:S(2)}) copy-start(f32[8,32,256]{2,1,0:T(8,128)} %param.18) | copy-start | bytes 786436
  2.6 12.2 %all-to-all-start = ((f32[8,1,8320]{2,1,0:T(1,128)}), f32[8,1,8320]{2,1,0:T(1,128)S(1)}, u32[]{:S(2)}, u32[]{:S(2)}) async-start(f32[8,1,8320]{2,1,0:T(1,128)} %bitcast.27), calls=%async_computation | async-start | bytes 532480 | tf_op jit(solution)/shard_map/all_to_all | solution.py:365
  8.6 1.0 copy-start.11
  16.1 50.2 %copy-start = (f32[2,256,256]{2,1,0:T(8,128)S(1)}, f32[2,256,256]{2,1,0:T(8,128)}, u32[]{:S(2)}) copy-start(f32[2,256,256]{2,1,0:T(8,128)} %constant.18.clone.xi_ref) | copy-start | bytes 1572868
  16.1 50.2 %copy-start.1 = (f32[2,256,256]{2,1,0:T(8,128)S(1)}, f32[2,256,256]{2,1,0:T(8,128)}, u32[]{:S(2)}) copy-start(f32[2,256,256]{2,1,0:T(8,128)} %constant.17.clone.yi_ref) | copy-start | bytes 1572868
  16.2 50.2 %copy-start.2 = (f32[2,256,256]{2,1,0:T(8,128)S(1)}, f32[2,256,256]{2,1,0:T(8,128)}, u32[]{:S(2)}) copy-start(f32[2,256,256]{2,1,0:T(8,128)} %constant.16.clone.yf_ref) | copy-start | bytes 1572868
  16.2 50.2 %copy-start.3 = (f32[2,256,256]{2,1,0:T(8,128)S(1)}, f32[2,256,256]{2,1,0:T(8,128)}, u32[]{:S(2)}) copy-start(f32[2,256,256]{2,1,0:T(8,128)} %constant.15.clone.xf_ref) | copy-start | bytes 1572868
  69.3 36.3 %copy-start.5 = (f32[2,256,256]{2,1,0:T(8,128)S(1)}, f32[2,256,256]{2,1,0:T(8,128)}, u32[]{:S(2)}) copy-start(f32[2,256,256]{2,1,0:T(8,128)} %constant.19.clone.table_ref) | copy-start | bytes 1572868
